TPU v7x, 32 devices: a whole 2x2x4 slice. The times are simulated.
32 devices in a mesh: grp: 2 (over y), path: 4 (over z), scen: 2 (over x), sub: 2 (over core).
Axes of the slice: x: 2, y: 2, z: 4, core: 2. Of those that a mesh axis runs over, the one named last changes fastest.
Arguments:
- path_links: int32 [8, 16384], P(None, ('grp', 'path')), parts along dimension 1, may hold values from -1 to 3583, as said below
- block_tiles: int32 [128, 16], P(('grp', 'path')), parts along dimension 0, may hold values from 0 to 27, as said below
- block_count: int32 [128], P(('grp', 'path')), parts along dimension 0, may hold values from 1 to 16
- path_commodity: int32 [128, 128], P(('grp', 'path')), parts along dimension 0, may hold values from 0 to 31, never falling along the last dimension, each value on 1 to 8 neighbouring positions
- demand: int32 [256, 4096], P(('scen', 'sub'), ('grp', 'path')), parts along dimension 1, may hold values from 1 to 64
- lengths: float32 [256, 7168], P(('scen', 'sub'), ('grp', 'path')), parts along dimension 1, may hold values from 0.05 to 10
- capacity: float32 [7168], P(('grp', 'path')), parts along dimension 0, may hold values from 4 to 32
- scenario_weight: float32 [512], P(('grp', 'scen', 'sub')), parts along dimension 0, may hold values from 0.5 to 2
Outputs:
- flows: float32 [256, 16384], P(('scen', 'sub'), ('grp', 'path')), parts along dimension 1
- lengths_next: float32 [256, 7168], P(('scen', 'sub'), ('grp', 'path')), parts along dimension 1
- robust_cost: float32 [16384], P(('grp', 'path')), parts along dimension 0
There are 2 independent parts, one for each index of `grp`. A program takes and returns all parts, laid end to end along the dimension named above; each array names one. Nothing has to cross between parts.
Inputs may be any that keep to these rules, and one draw needn't show every extreme that they name: `path_links`: entry [h, p] is the link of hop h of path p, or -1 past the path's last hop (hop 0 is never -1). Every link of a path in block b = p // 128 lies in a link block named by block_tiles[b, 0] to block_tiles[b, block_count[b] - 1]; link block j holds links j * 128 to (j + 1) * 128 - 1. `block_tiles`: the entries of one row are distinct link blocks.
All inputs are finite; a program needn't handle non-finite values.
Results may differ from a plain program's by a relative error of at most 0.0003.
Values sent between devices are 32-bit elements; how exact they have to be, the bound alone decides.
No kernel may reach another device: no remote copies, remote signals or barrier semaphores. Data moves between devices by JAX's collectives and lax.ppermute only.
A program may use at most 64 MiB of HBM per device.

v0:
```python
import jax
import jax.numpy as jnp
from jax import lax
from jax.sharding import PartitionSpec as P

PATHS_PER_BLOCK = 128
LB = 128
MAXT = 16
COMMODITY_BLOCK = 32
S = 256
SOFTMIN_RATE = 0.25
STEP_RATE = 1.0
DEMAND_UNIT = 0.0625
PRECISE = lax.Precision.HIGHEST


def incidence(hop_links, tile_ids, live_count):
    link_block = hop_links // LB
    column = hop_links % LB
    live_slots = jnp.arange(MAXT) < live_count
    slot_match = (
        (link_block[:, :, None] == tile_ids[None, None, :]) & live_slots[None, None, :]
    ).astype(jnp.float32)
    column_hot = (column[:, :, None] == jnp.arange(LB)[None, None, :]).astype(jnp.float32)
    return jnp.einsum("hpt,hpl->ptl", slot_match, column_hot, precision=PRECISE)


def tile_costs(table_grid, tile_ids, tile_hits):
    chosen = jnp.take(table_grid, tile_ids, axis=1)
    return jnp.einsum("stl,ptl->sp", chosen, tile_hits, precision=PRECISE)


def tile_loads(block_flow, tile_hits):
    return jnp.einsum("sp,ptl->stl", block_flow, tile_hits, precision=PRECISE)


def block_flows(block_cost, commodity_id, block_demand):
    commodity_onehot = (commodity_id[:, None] == jnp.arange(COMMODITY_BLOCK)[None, :]).astype(
        jnp.float32
    )
    weight = jnp.exp(-SOFTMIN_RATE * block_cost)
    totals = jnp.dot(
        weight, commodity_onehot, preferred_element_type=jnp.float32, precision=PRECISE
    )
    per_path = jnp.dot(
        totals, commodity_onehot.T, preferred_element_type=jnp.float32, precision=PRECISE
    )
    wanted = jnp.dot(
        block_demand.astype(jnp.float32) * DEMAND_UNIT,
        commodity_onehot.T,
        preferred_element_type=jnp.float32,
        precision=PRECISE,
    )
    return wanted * weight / per_path


def flow_sweep(length_wide, links_by_block, tile_table, count_table, comm_table, block_demands):
    scenario_rows = length_wide.shape[0]
    length_grid = length_wide.reshape(scenario_rows, -1, LB)

    def first_pass(load_grid, pieces):
        hop_links, tile_ids, live_count, commodity_id, block_demand = pieces
        tile_hits = incidence(hop_links, tile_ids, live_count)
        block_cost = tile_costs(length_grid, tile_ids, tile_hits)
        block_flow = block_flows(block_cost, commodity_id, block_demand)
        load_grid = load_grid.at[:, tile_ids, :].add(tile_loads(block_flow, tile_hits))
        return (load_grid, block_flow)

    load_grid, flow_blocks = lax.scan(
        first_pass,
        jnp.zeros(length_grid.shape, jnp.float32),
        (links_by_block, tile_table, count_table, comm_table, block_demands),
    )
    flows = flow_blocks.transpose(1, 0, 2).reshape(scenario_rows, -1)
    return (flows, load_grid.reshape(scenario_rows, -1))


def cost_sweep(next_wide, weight_rows, links_by_block, tile_table, count_table):
    scenario_rows = next_wide.shape[0]
    next_grid = next_wide.reshape(scenario_rows, -1, LB)

    def second_pass(carried, pieces):
        hop_links, tile_ids, live_count = pieces
        tile_hits = incidence(hop_links, tile_ids, live_count)
        block_cost = tile_costs(next_grid, tile_ids, tile_hits)
        mixed = (
            jnp.dot(
                weight_rows[None, :],
                block_cost,
                preferred_element_type=jnp.float32,
                precision=PRECISE,
            )[0]
            / S
        )
        return (carried, mixed)

    _, partial_value = lax.scan(
        second_pass, jnp.zeros((), jnp.float32), (links_by_block, tile_table, count_table)
    )
    return partial_value.reshape(-1)


def body(
    path_links, block_tiles, block_count, path_commodity, demand, lengths, capacity, scenario_weight
):
    hop_count, path_total = path_links.shape
    block_list = block_tiles.shape[0]
    scenario_rows, link_rows = lengths.shape
    links_by_block = path_links.reshape(hop_count, block_list, PATHS_PER_BLOCK).transpose(1, 0, 2)
    block_demands = demand.reshape(scenario_rows, block_list, COMMODITY_BLOCK).transpose(1, 0, 2)
    gathered = lax.all_gather(lengths, "path", axis=1, tiled=True)
    flows, load_full = flow_sweep(
        gathered, links_by_block, block_tiles, block_count, path_commodity, block_demands
    )
    link_total = gathered.shape[1]
    own_loads = lax.psum_scatter(load_full, "path", scatter_dimension=1, tiled=True)
    grown_len = lengths * jnp.exp(STEP_RATE * own_loads / capacity[None, :])
    totals = lax.psum(jnp.sum(grown_len, axis=1), "path")
    lengths_next = grown_len * (link_total / totals)[:, None]
    wide_next = lax.all_gather(lengths_next, "path", axis=1, tiled=True)
    partial_value = cost_sweep(wide_next, scenario_weight, links_by_block, block_tiles, block_count)
    robust = lax.psum(partial_value, ("scen", "sub"))
    return (flows, lengths_next, robust)


def solution(mesh):
    return jax.shard_map(
        body,
        mesh=mesh,
        in_specs=(
            P(None, ("grp", "path")),
            P(("grp", "path"), None),
            P(("grp", "path")),
            P(("grp", "path"), None),
            P(("scen", "sub"), ("grp", "path")),
            P(("scen", "sub"), ("grp", "path")),
            P(("grp", "path")),
            P(("grp", "scen", "sub")),
        ),
        out_specs=(
            P(("scen", "sub"), ("grp", "path")),
            P(("scen", "sub"), ("grp", "path")),
            P(("grp", "path")),
        ),
        check_vma=False,
    )
```

profile of v0, /device:TPU:0, one launch (start us, length us, event | category | flops | bytes accessed | tf_op | source)
XLA Modules:
  0.0 389.9 jit_solution(973819889943569372)
XLA Ops:
  7.2 23.0 %all_gather.6 = f32[64,3584]{1,0:T(8,128)S(1)} all-gather(f32[64,896]{1,0:T(8,128)} %param.19), channel_id=1, replica_groups=mesh['grp'=2,'path'=4,'scen'=2,'sub'=2] {'path'}, dimensions={1}, use_global_device_ids=true | all-gather | bytes 1146880 | tf_op jit(solution)/shard_map/all_gather | solution.py:111
  32.6 185.0 %while.26 = (s32[]{:T(128)}, f32[64,28,128]{2,0,1:T(8,128)S(1)}, f32[16,64,128]{2,1,0:T(8,128)}, s32[16,16]{1,0:T(8,128)}, s32[16,64,32]{1,2,0:T(8,128)}, /*inde...) while((s32[]{:T(128)}, f32[64,28,128]{2,0,1:T(8,128)S(1)}, ...), condition=%wide.region_2.4_spmd, body=%wide.region_0.3_spmd.sunk | while | flops 416772288 | bytes 7180105 | solution.py:69
  33.2 1.3 compare_and_fusion.6
  36.8 1.4 fusion.88
  42.8 1.3 scatter_fusion
  44.7 1.3 compare_and_fusion.6
  48.3 1.4 fusion.88
  56.3 1.3 compare_and_fusion.6
  59.9 1.4 fusion.88
  67.9 1.3 compare_and_fusion.6
  71.5 1.4 fusion.88
  77.5 1.3 scatter_fusion
  79.4 1.3 compare_and_fusion.6
  83.0 1.4 fusion.88
  89.0 1.3 scatter_fusion
  91.0 1.3 compare_and_fusion.6
  94.6 1.4 fusion.88
  102.5 1.3 compare_and_fusion.6
  106.2 1.4 fusion.88
  114.1 1.3 compare_and_fusion.6
  117.7 1.4 fusion.88
  123.7 1.3 scatter_fusion
  125.7 1.3 compare_and_fusion.6
  129.3 1.4 fusion.88
  135.3 1.3 scatter_fusion
  137.3 1.3 compare_and_fusion.6
  140.9 1.4 fusion.88
  146.9 1.3 scatter_fusion
  148.8 1.3 compare_and_fusion.6
  152.4 1.4 fusion.88
  158.4 1.3 scatter_fusion
  160.4 1.3 compare_and_fusion.6
  164.0 1.4 fusion.88
  170.0 1.3 scatter_fusion
  171.9 1.3 compare_and_fusion.6
  175.6 1.4 fusion.88
  181.6 1.3 scatter_fusion
  183.5 1.3 compare_and_fusion.6
  187.1 1.4 fusion.88
  195.1 1.3 compare_and_fusion.6
  198.7 1.4 fusion.88
  206.6 1.3 compare_and_fusion.6
  210.3 1.4 fusion.88
  220.5 23.0 %reduce-scatter.2.cloned.1.call-done = f32[64,896]{1,0:T(8,128)} async-done(((f32[64,3584]{1,0:T(8,128)}), f32[64,896]{1,0:T(8,128)}) %reduce-scatter.2.cloned.1.call-update) | async-done | bytes 229392 | tf_op jit(solution)/shard_map/reduce_scatter | solution.py:116
  244.6 9.7 %psum.14 = f32[64]{0:T(128)S(1)} all-reduce(f32[64]{0:T(128)S(1)} %fusion.47), channel_id=1, replica_groups=mesh['grp'=2,'path'=4,'scen'=2,'sub'=2] {'path'}, use_global_device_ids=true, to_apply=%region_5.7 | all-reduce | flops 64 | bytes 512 | tf_op jit(solution)/shard_map/psum | solution.py:118
  254.5 18.4 %all_gather.7 = f32[64,3584]{1,0:T(8,128)S(1)} all-gather(f32[64,896]{1,0:T(8,128)S(1)} %broadcast_multiply_fusion), channel_id=1, replica_groups=mesh['grp'=2,'path'=4,'scen'=2,'sub'=2] {'path'}, dimensions={1}, use_global_device_ids=true | all-gather | bytes 1146880 | tf_op jit(solution)/shard_map/all_gather | solution.py:120
  273.5 103.2 %while.27 = (s32[]{:T(128)}, f32[16,128]{1,0:T(8,128)S(1)}, s32[16,16]{1,0:T(8,128)}, f32[64,28,128]{2,0,1:T(8,128)S(1)}, s32[16,8,128]{2,1,0:T(8,128)}, /*index...) while((s32[]{:T(128)}, f32[16,128]{1,0:T(8,128)S(1)}, s32[16,16]{1,0:T(8,128)}, ...), condition=%wide.region_7.9_spmd, body=%wide.region_6.8_spmd.sunk | while | flops 205941024 | bytes 4063613 | solution.py:97
  278.4 1.4 convolution_bitcast_fusion.7
  284.8 1.4 convolution_bitcast_fusion.7
  291.3 1.4 convolution_bitcast_fusion.7
  297.7 1.4 convolution_bitcast_fusion.7
  304.2 1.4 convolution_bitcast_fusion.7
  310.6 1.4 convolution_bitcast_fusion.7
  317.1 1.4 convolution_bitcast_fusion.7
  323.5 1.4 convolution_bitcast_fusion.7
  330.0 1.4 convolution_bitcast_fusion.7
  336.4 1.4 convolution_bitcast_fusion.7
  342.9 1.4 convolution_bitcast_fusion.7
  349.3 1.4 convolution_bitcast_fusion.7
  355.8 1.4 convolution_bitcast_fusion.7
  362.2 1.4 convolution_bitcast_fusion.7
  368.7 1.4 convolution_bitcast_fusion.7
  375.1 1.4 convolution_bitcast_fusion.7
  376.7 6.3 %psum.15 = f32[2048]{0:T(1024)} all-reduce(f32[2048]{0:T(1024)S(1)} %bitcast.175), channel_id=1, replica_groups=mesh['grp'=2,'path'=4,'scen'=2,'sub'=2] {'scen','sub'}, use_global_device_ids=true, to_apply=%region_8.10 | all-reduce | flops 2048 | bytes 16384 | tf_op jit(solution)/shard_map/psum | solution.py:122
  (484 shorter events, 215.4 us)
Async XLA Ops:
  7.2 236.3 %reduce-scatter.2.cloned.1.call-start = ((), (), s32[]{:S(2)}) async-start(), calls=%async_computation.1 | async-start | bytes 1146880 | tf_op jit(solution)/shard_map/reduce_scatter | solution.py:116
  30.2 0.9 copy-start.4
  31.9 0.7 copy-start.7
  218.6 1.0 copy-start.3
  219.7 23.8 %copy-start = (f32[64,896]{1,0:T(8,128)S(1)}, f32[64,896]{1,0:T(8,128)}, u32[]{:S(2)}) copy-start(f32[64,896]{1,0:T(8,128)} %param.19) | copy-start | bytes 688132
  219.7 23.8 %copy-start.5 = (f32[896]{0:T(1024)S(1)}, f32[896]{0:T(1024)}, u32[]{:S(2)}) copy-start(f32[896]{0:T(1024)} %param.20) | copy-start | bytes 10756
  243.5 10.9 %copy-start.1 = (f32[64,896]{1,0:T(8,128)S(1)}, f32[64,896]{1,0:T(8,128)}, u32[]{:S(2)}) copy-start(f32[64,896]{1,0:T(8,128)} %reduce-scatter.2.cloned.1.call-done) | copy-start | bytes 688132
  254.4 18.4 %copy-start.2 = (f32[64,896]{1,0:T(8,128)}, f32[64,896]{1,0:T(8,128)S(1)}, u32[]{:S(2)}) copy-start(f32[64,896]{1,0:T(8,128)S(1)} %broadcast_multiply_fusion) | copy-start | bytes 688132
  272.8 0.7 copy-start.6
Sparse Core Ops, SparseCore 0:
  218.8 24.6 reduce-scatter.1
where the time goes:
time: 395 us; the launch traced here: 390 us
  other arithmetic  106 us (27%)
  matrix products  106 us (27%)
  local copies, waits for them, and re-layouts  80.8 us (20%)
  blocking collectives  57.4 us (15%)
  waiting for transfers between devices  23 us (6%)
  between operations  14.1 us (4%)
    dynamic_slice x96, local copies, waits for them, and re-layouts, flow_sweep(): lax.scan(first_pass, jnp.zeros(length_grid.shape, jnp.float32), (links_by...  44.7 us
    dot_general x32, matrix products, tile_costs(): return jnp.einsum('stl,ptl->sp', chosen, tile_hits, precision=PRECISE)  44.3 us
    and x32, other arithmetic, tile_costs(): chosen = jnp.take(table_grid, tile_ids, axis=1)  42.4 us
    reduce_scatter x1, waiting for transfers between devices, body(): lax.psum_scatter(load_full, 'path', scatter_dimension=1, tiled=True)  23 us
    all_gather x1, blocking collectives, body(): gathered = lax.all_gather(lengths, 'path', axis=1, tiled=True)  23 us
    scatter-add x16, other arithmetic, first_pass(): load_grid.at[:, tile_ids, :].add(tile_loads(block_flow, tile_hits))  21.2 us
    dot_general x32, matrix products, incidence(): return jnp.einsum('hpt,hpl->ptl', slot_match, column_hot, precision=PRECISE)  21.2 us
    gather x32, local copies, waits for them, and re-layouts, tile_costs(): chosen = jnp.take(table_grid, tile_ids, axis=1)  18.6 us
  transfers between devices with their start and end apart: 1, of which 1 were waited for; matrix products, arithmetic and copies ran while one was open for 0% of the time, Pallas kernels for 0%

commit v1 on v0

--- a/solution.py
+++ b/solution.py
@@ -1,3 +1,4 @@
+import functools
 import jax
 import jax.numpy as jnp
 from jax import lax
@@ -12,6 +13,15 @@
 STEP_RATE = 1.0
 DEMAND_UNIT = 0.0625
 PRECISE = lax.Precision.HIGHEST
+
+
+def convert_region(x_in, axis_id):
+    high = lax.all_gather(x_in, axis_name=axis_id)
+    reply = jnp.sum(high, axis=0)
+    return reply
+
+
+_apply_slots = functools.partial(convert_region, axis_id="path")
 
 
 def incidence(hop_links, tile_ids, live_count):
@@ -115,7 +125,7 @@
     link_total = gathered.shape[1]
     own_loads = lax.psum_scatter(load_full, "path", scatter_dimension=1, tiled=True)
     grown_len = lengths * jnp.exp(STEP_RATE * own_loads / capacity[None, :])
-    totals = lax.psum(jnp.sum(grown_len, axis=1), "path")
+    totals = _apply_slots(jnp.sum(grown_len, axis=1))
     lengths_next = grown_len * (link_total / totals)[:, None]
     wide_next = lax.all_gather(lengths_next, "path", axis=1, tiled=True)
     partial_value = cost_sweep(wide_next, scenario_weight, links_by_block, block_tiles, block_count)

time: 395 us -> 418 us (1.058)
  other arithmetic: 106 us -> 133 us
  local copies, waits for them, and re-layouts: 80.8 us -> 70.5 us
  matrix products: 106 us -> 111 us
    select_n x16 -> x32, other arithmetic: 11.2 us -> 28.1 us  [incidence(): column = hop_links % LB]
    select_n x32, other arithmetic: 12.1 us -> 28.4 us  [incidence(): link_block = hop_links // LB]
    dynamic_slice x96 -> x64, local copies, waits for them, and re-layouts: 44.7 us -> 31.6 us  [flow_sweep(): lax.scan(first_pass, jnp.zeros(length_grid.shape, jnp.float32), (links_by...]
    psum x1 -> x0, blocking collectives: 9.72 us -> none  [body(): totals = lax.psum(jnp.sum(grown_len, axis=1), 'path')]
    unnamed x0 -> x1, blocking collectives: none -> 9.68 us
    dot_general x32, matrix products: 21.2 us -> 25.8 us  [incidence(): return jnp.einsum('hpt,hpl->ptl', slot_match, column_hot, precision=PRECISE)]
where the time goes in v1:
time: 418 us; the launch traced here: 411 us
  other arithmetic  133 us (32%)
  matrix products  111 us (27%)
  local copies, waits for them, and re-layouts  70.5 us (17%)
  blocking collectives  57.1 us (14%)
  waiting for transfers between devices  22 us (5%)
  between operations  14.8 us (4%)
    dot_general x32, matrix products, tile_costs(): return jnp.einsum('stl,ptl->sp', chosen, tile_hits, precision=PRECISE)  44.4 us
    and x32, other arithmetic, tile_costs(): chosen = jnp.take(table_grid, tile_ids, axis=1)  43 us
    dynamic_slice x64, local copies, waits for them, and re-layouts, flow_sweep(): lax.scan(first_pass, jnp.zeros(length_grid.shape, jnp.float32), (links_by...  31.6 us
    select_n x32, other arithmetic, incidence(): link_block = hop_links // LB  28.4 us
    select_n x32, other arithmetic, incidence(): column = hop_links % LB  28.1 us
    dot_general x32, matrix products, incidence(): return jnp.einsum('hpt,hpl->ptl', slot_match, column_hot, precision=PRECISE)  25.8 us
    all_gather x1, blocking collectives, body(): gathered = lax.all_gather(lengths, 'path', axis=1, tiled=True)  22.7 us
    reduce_scatter x1, waiting for transfers between devices, body(): lax.psum_scatter(load_full, 'path', scatter_dimension=1, tiled=True)  22 us
  transfers between devices with their start and end apart: 1, of which 1 were waited for; matrix products, arithmetic and copies ran while one was open for 0% of the time, Pallas kernels for 0%

profile of v1, /device:TPU:0, one launch (start us, length us, event | category | flops | bytes accessed | tf_op | source)
XLA Modules:
  0.0 411.4 jit_solution(376771118940815321)
XLA Ops:
  7.2 2.2 copy.30
  9.4 22.7 %all_gather.12 = f32[64,3584]{1,0:T(8,128)S(1)} all-gather(f32[64,896]{1,0:T(8,128)S(1)} %copy-done), channel_id=1, replica_groups=mesh['grp'=2,'path'=4,'scen'=2,'sub'=2] {'path'}, dimensions={1}, use_global_device_ids=true | all-gather | bytes 1146880 | tf_op jit(solution)/shard_map/all_gather | solution.py:121
  34.6 200.3 %while.26 = (s32[]{:T(128)}, f32[64,28,128]{2,0,1:T(8,128)S(1)}, f32[16,64,128]{2,1,0:T(8,128)}, s32[16,16]{1,0:T(8,128)}, s32[16,64,32]{1,2,0:T(8,128)}, /*inde...) while((s32[]{:T(128)}, f32[64,28,128]{2,0,1:T(8,128)S(1)}, ...), condition=%wide.region_2.4_spmd, body=%wide.region_0.3_spmd.sunk | while | flops 416778432 | bytes 7169869 | solution.py:79
  35.1 1.3 compare_and_fusion.4
  39.7 1.4 fusion.90
  47.7 1.3 compare_and_fusion.4
  52.2 1.4 fusion.90
  60.2 1.3 compare_and_fusion.4
  64.7 1.4 fusion.90
  72.7 1.3 compare_and_fusion.4
  77.2 1.4 fusion.90
  85.2 1.3 compare_and_fusion.4
  89.8 1.4 fusion.90
  97.7 1.3 compare_and_fusion.4
  102.3 1.4 fusion.90
  110.3 1.3 compare_and_fusion.4
  114.8 1.4 fusion.90
  122.8 1.3 compare_and_fusion.4
  127.3 1.4 fusion.90
  135.3 1.3 compare_and_fusion.4
  139.8 1.4 fusion.90
  147.8 1.3 compare_and_fusion.4
  152.3 1.4 fusion.90
  160.3 1.3 compare_and_fusion.4
  164.9 1.4 fusion.90
  172.8 1.3 compare_and_fusion.4
  177.4 1.4 fusion.90
  185.4 1.3 compare_and_fusion.4
  189.9 1.4 fusion.90
  197.9 1.3 compare_and_fusion.4
  202.4 1.4 fusion.90
  214.9 1.4 fusion.90
  227.4 1.4 fusion.90
  238.7 22.0 %reduce-scatter.2.cloned.1.call-done = f32[64,896]{1,0:T(8,128)} async-done(((f32[64,3584]{1,0:T(8,128)}), f32[64,896]{1,0:T(8,128)}) %reduce-scatter.2.cloned.1.call-update) | async-done | bytes 229392 | tf_op jit(solution)/shard_map/reduce_scatter | solution.py:126
  262.2 9.7 %all-reduce = f32[256]{0:T(256)S(1)} all-reduce(f32[256]{0:T(256)S(1)} %dynamic-update-slice), channel_id=2, replica_groups=mesh['grp'=2,'path'=4,'scen'=2,'sub'=2] {'path'}, use_global_device_ids=true, to_apply=%add | all-reduce | flops 256 | bytes 2048
  272.1 18.4 %all_gather.15 = f32[64,3584]{1,0:T(8,128)S(1)} all-gather(f32[64,896]{1,0:T(8,128)S(1)} %broadcast_multiply_fusion), channel_id=1, replica_groups=mesh['grp'=2,'path'=4,'scen'=2,'sub'=2] {'path'}, dimensions={1}, use_global_device_ids=true | all-gather | bytes 1146880 | tf_op jit(solution)/shard_map/all_gather | solution.py:130
  291.1 107.1 %while.27 = (s32[]{:T(128)}, f32[16,128]{1,0:T(8,128)S(1)}, s32[16,16]{1,0:T(8,128)}, f32[64,28,128]{2,0,1:T(8,128)S(1)}, s32[16,8,128]{1,2,0:T(8,128)}, /*index...) while((s32[]{:T(128)}, f32[16,128]{1,0:T(8,128)S(1)}, s32[16,16]{1,0:T(8,128)}, ...), condition=%wide.region_7.9_spmd, body=%wide.region_6.8_spmd.sunk | while | flops 205941024 | bytes 3768701 | solution.py:107
  293.4 1.3 compare_and_fusion.5
  296.2 1.4 convolution_bitcast_fusion.7
  302.9 1.4 convolution_bitcast_fusion.7
  309.6 1.4 convolution_bitcast_fusion.7
  313.5 1.3 compare_and_fusion.5
  316.3 1.4 convolution_bitcast_fusion.7
  320.2 1.3 compare_and_fusion.5
  323.0 1.4 convolution_bitcast_fusion.7
  326.9 1.3 compare_and_fusion.5
  329.7 1.4 convolution_bitcast_fusion.7
  336.4 1.4 convolution_bitcast_fusion.7
  340.3 1.3 compare_and_fusion.5
  343.1 1.4 convolution_bitcast_fusion.7
  347.0 1.3 compare_and_fusion.5
  349.8 1.4 convolution_bitcast_fusion.7
  353.7 1.3 compare_and_fusion.5
  356.5 1.4 convolution_bitcast_fusion.7
  363.2 1.4 convolution_bitcast_fusion.7
  369.9 1.4 convolution_bitcast_fusion.7
  373.8 1.3 compare_and_fusion.5
  376.6 1.4 convolution_bitcast_fusion.7
  380.5 1.3 compare_and_fusion.5
  383.3 1.4 convolution_bitcast_fusion.7
  387.2 1.3 compare_and_fusion.5
  390.0 1.4 convolution_bitcast_fusion.7
  396.7 1.4 convolution_bitcast_fusion.7
  398.2 6.3 %psum.7 = f32[2048]{0:T(1024)} all-reduce(f32[2048]{0:T(1024)S(1)} %bitcast.174), channel_id=1, replica_groups=mesh['grp'=2,'path'=4,'scen'=2,'sub'=2] {'scen','sub'}, use_global_device_ids=true, to_apply=%region_8.10 | all-reduce | flops 2048 | bytes 16384 | tf_op jit(solution)/shard_map/psum | solution.py:132
  (446 shorter events, 236.7 us)
Async XLA Ops:
  7.2 253.6 %reduce-scatter.2.cloned.1.call-start = ((), (), s32[]{:S(2)}) async-start(), calls=%async_computation.1 | async-start | bytes 1146880 | tf_op jit(solution)/shard_map/reduce_scatter | solution.py:126
  7.2 2.2 copy-start
  32.2 0.9 copy-start.5
  33.9 0.7 copy-start.8
  235.9 2.0 copy-start.4
  235.9 0.7 copy-start.9
  237.9 22.8 %copy-start.1 = (f32[64,896]{1,0:T(8,128)S(1)}, f32[64,896]{1,0:T(8,128)}, u32[]{:S(2)}) copy-start(f32[64,896]{1,0:T(8,128)} %param.19) | copy-start | bytes 688132
  237.9 22.8 %copy-start.6 = (f32[896]{0:T(1024)S(1)}, f32[896]{0:T(1024)}, u32[]{:S(2)}) copy-start(f32[896]{0:T(1024)} %param.20) | copy-start | bytes 10756
  260.7 11.2 %copy-start.2 = (f32[64,896]{1,0:T(8,128)S(1)}, f32[64,896]{1,0:T(8,128)}, u32[]{:S(2)}) copy-start(f32[64,896]{1,0:T(8,128)} %reduce-scatter.2.cloned.1.call-done) | copy-start | bytes 688132
  272.1 18.4 %copy-start.3 = (f32[64,896]{1,0:T(8,128)}, f32[64,896]{1,0:T(8,128)S(1)}, u32[]{:S(2)}) copy-start(f32[64,896]{1,0:T(8,128)S(1)} %broadcast_multiply_fusion) | copy-start | bytes 688132
  290.4 0.7 copy-start.7
Sparse Core Ops, SparseCore 0:
  236.0 24.6 reduce-scatter.1
